TPU v7x, 256 devices: a whole 4x4x8 slice. The times are simulated.
256 devices in a mesh: dp: 32 (over y, z), mp: 8 (over x, core).
Axes of the slice: x: 4, y: 4, z: 8, core: 2. Of those that a mesh axis runs over, the one named last changes fastest.
Arguments:
- tokens: bfloat16 [8192, 2048], P('dp'), may hold values from -6 to 6
- out_grad: bfloat16 [8192, 2048], P('dp'), may hold values from -6 to 6
- master: float32 [2240, 3, 7168], P('dp', None, 'mp'), may hold values from -6 to 6
- moment_one: float32 [2240, 3, 7168], P('dp', None, 'mp'), may hold values from -6 to 6
- moment_two: float32 [2240, 3, 7168], P('dp', None, 'mp'), may hold values from 0.05 to 5
- old_offsets: int32 [33], replicated, may hold values from 0 to 2048, as said below
- new_offsets: int32 [33], replicated, may hold values from 0 to 2048, as said below
Outputs:
- new_master: float32 [2752, 3, 7168], P('dp', None, 'mp')
- new_moment_one: float32 [2752, 3, 7168], P('dp', None, 'mp')
- new_moment_two: float32 [2752, 3, 7168], P('dp', None, 'mp')
- layer_output: bfloat16 [8192, 2048], P('dp', 'mp')
Inputs may be any that keep to these rules, and one draw needn't show every extreme that they name: non-decreasing, old_offsets[0] = 0 and old_offsets[32] = 2048; device p holds rows old_offsets[p] to old_offsets[p + 1] - 1 in its first slots; every device holds at least one and at most 70 rows, and some device exactly 70. non-decreasing, new_offsets[0] = 0 and new_offsets[32] = 2048; exactly one device holds no rows, its index at least 2 and at most 15; every other device holds at least one and at most 86 rows, some device exactly 86; a row's device in the new layout is its device in the old layout or the next one along dp.
All inputs are finite; a program needn't handle non-finite values.
Results may differ from a plain program's by a relative error of at most 0.014.
Values may be sent and summed in bfloat16 or wider, within the bound.
No kernel may reach another device: no remote copies, remote signals or barrier semaphores. Data moves between devices by JAX's collectives and lax.ppermute only.
A program may use at most 128 MiB of HBM per device.

v0:
```python
import jax
import jax.numpy as jnp
from jax import lax
from jax.sharding import PartitionSpec as P

FEATURE_WIDTH = 2048
FF = 7168
beta_one = 0.9
beta_two = 0.95
learn_rate = 0.01
decay_rate = 0.1
adam_eps = 1e-08
bias_one = 1.0 - 0.9**10
bias_two = 1.0 - 0.95**10


def passed_along(value, axis, by):
    peers = lax.axis_size(axis)
    pairs = [(i, i + by) for i in range(peers) if 0 <= i + by < peers]
    return lax.ppermute(value, axis, pairs)


def lookup(small_table, wanted):
    matches = wanted[..., None] == jnp.arange(small_table.shape[0], dtype=jnp.int32)
    return jnp.sum(jnp.where(matches, small_table, 0), axis=-1)


def row_layout(row_count, capacity, offsets):
    row_index = jnp.arange(row_count, dtype=jnp.int32)
    owner_index = row_index // capacity
    local_index = row_index - owner_index * capacity
    row_start = lookup(offsets, owner_index)
    in_range = local_index < lookup(offsets, owner_index + 1) - row_start
    target = jnp.clip(row_start + local_index, 0, FEATURE_WIDTH - 1)
    return (target, in_range)


def adam_step(master_rows, first_rows, second_rows, grads):
    first_new = beta_one * first_rows + (1.0 - beta_one) * grads
    second_new = beta_two * second_rows + (1.0 - beta_two) * grads * grads
    update = first_new / bias_one / (jnp.sqrt(second_new / bias_two) + adam_eps)
    master_new = master_rows - learn_rate * (update + decay_rate * master_rows)
    return (master_new, first_new, second_new)


def reshard(states, old_offsets, new_offsets, capacity_new):
    capacity_old = states.shape[0]
    from_left = passed_along(states.astype(jnp.bfloat16), "dp", 1).astype(states.dtype)
    device_index = lax.axis_index("dp")
    local_index = jnp.arange(capacity_new, dtype=jnp.int32)
    row_start = lookup(new_offsets, device_index)
    row_count = lookup(new_offsets, device_index + 1) - row_start
    in_range = local_index < row_count
    row_index = jnp.clip(row_start + local_index, 0, FEATURE_WIDTH - 1)
    owner_index = jnp.sum(
        (old_offsets[1:-1][None, :] <= row_index[:, None]).astype(jnp.int32), axis=1
    )
    slot_index = (
        (owner_index - device_index + 1) * capacity_old
        + row_index
        - lookup(old_offsets, owner_index)
    )
    neighbours = jnp.concatenate([from_left, states], axis=0)
    picked = jnp.take(neighbours, slot_index, axis=0, mode="clip")
    return jnp.where(in_range[:, None, None, None], picked, 0.0)


def train_pass(tokens, upstream, weights, layout, capacity, live_flag):
    columns = weights.shape[2]
    scale_in = FEATURE_WIDTH ** (-0.5)
    scale_hidden = FF ** (-0.5)
    contract_rows = (((0,), (0,)), ((), ()))
    shard_piece = lax.all_gather(weights, "dp", axis=0, tiled=True)
    down_rows = jnp.zeros((FEATURE_WIDTH, columns), jnp.bfloat16)
    target, in_range = row_layout(shard_piece.shape[0], capacity, layout)
    shard_piece = jnp.where(in_range[:, None, None], shard_piece, jnp.zeros_like(shard_piece))
    token_columns = jnp.take(tokens, target, axis=1, mode="clip")
    upstream_columns = jnp.take(upstream, target, axis=1, mode="clip")
    gate_sum = jnp.dot(token_columns, shard_piece[:, 0], preferred_element_type=jnp.float32)
    up_sum = jnp.dot(token_columns, shard_piece[:, 1], preferred_element_type=jnp.float32)
    back_sum = jnp.dot(upstream_columns, shard_piece[:, 2], preferred_element_type=jnp.float32)
    placed = jnp.where(in_range, target, FEATURE_WIDTH)
    down_rows = down_rows.at[placed].set(shard_piece[:, 2], mode="drop")
    gate_sum, up_sum, back_sum, down_rows = (gate_sum, up_sum, back_sum, down_rows)
    gate_act = gate_sum * scale_in
    up_act = up_sum * scale_in
    back_grad = back_sum * scale_hidden
    sigmoid_gate = jax.nn.sigmoid(gate_act)
    hidden = (gate_act * sigmoid_gate * up_act).astype(jnp.bfloat16)
    partial_value = (
        lax.dot_general(
            hidden, down_rows, (((1,), (1,)), ((), ())), preferred_element_type=jnp.float32
        )
        * scale_hidden
    )
    partial_value = jnp.where(live_flag, partial_value, 0.0)
    layer_output = lax.psum_scatter(
        partial_value.astype(jnp.bfloat16), "mp", scatter_dimension=1, tiled=True
    )
    gate_grad = (
        back_grad * up_act * sigmoid_gate * (1.0 + gate_act * (1.0 - sigmoid_gate))
    ).astype(jnp.bfloat16)
    up_grad = (back_grad * gate_act * sigmoid_gate).astype(jnp.bfloat16)
    target, in_range = row_layout(lax.axis_size("dp") * capacity, capacity, layout)
    token_columns = jnp.take(tokens, target, axis=1, mode="clip")
    upstream_columns = jnp.take(upstream, target, axis=1, mode="clip")
    gate_part = (
        lax.dot_general(token_columns, gate_grad, contract_rows, preferred_element_type=jnp.float32)
        * scale_in
    )
    up_part = (
        lax.dot_general(token_columns, up_grad, contract_rows, preferred_element_type=jnp.float32)
        * scale_in
    )
    down_part = (
        lax.dot_general(upstream_columns, hidden, contract_rows, preferred_element_type=jnp.float32)
        * scale_hidden
    )
    stacked = jnp.stack([gate_part, up_part, down_part], axis=1)
    grads = lax.psum_scatter(
        jnp.where(in_range[:, None, None], stacked, 0.0).astype(jnp.bfloat16),
        "dp",
        scatter_dimension=0,
        tiled=True,
    ).astype(jnp.float32)
    return (grads, layer_output)


def body(tokens, out_grad, master, moment_one, moment_two, old_offsets, new_offsets):
    devices = lax.axis_size("dp")
    shard_rows = FEATURE_WIDTH // devices
    jitter_rows = shard_rows // (2 * (devices - 1)) + 2
    capacity_new = shard_rows + shard_rows // 4 + 2 * jitter_rows
    device_index = lax.axis_index("dp")
    live_flag = lookup(new_offsets, device_index + 1) != lookup(new_offsets, device_index)
    upstream = jnp.where(live_flag, out_grad, jnp.zeros_like(out_grad))
    states = jnp.stack([master, moment_one, moment_two], axis=1)
    states = reshard(states, old_offsets, new_offsets, capacity_new)
    weights = states[:, 0].astype(jnp.bfloat16)
    grads, layer_output = train_pass(
        tokens, upstream, weights, new_offsets, states.shape[0], live_flag
    )
    updated = jnp.stack(adam_step(states[:, 0], states[:, 1], states[:, 2], grads), axis=1)
    return (updated[:, 0], updated[:, 1], updated[:, 2], layer_output)


def solution(mesh):
    placed = (
        P("dp", None),
        P("dp", None),
        P("dp", None, "mp"),
        P("dp", None, "mp"),
        P("dp", None, "mp"),
        P(),
        P(),
    )
    return jax.shard_map(
        body,
        mesh=mesh,
        in_specs=placed,
        out_specs=(P("dp", None, "mp"), P("dp", None, "mp"), P("dp", None, "mp"), P("dp", "mp")),
        check_vma=False,
    )
```

profile of v0, /device:TPU:8, one launch (start us, length us, event | category | flops | bytes accessed | tf_op | source)
XLA Modules:
  0.0 586.7 jit_solution(979489931884639020)
XLA Ops:
  7.2 3.0 maximum_convert_fusion
  10.2 3.8 collective-permute-start
  14.1 0.7 slice.23
  14.8 1.3 fusion.27
  18.1 0.7 select_reduce_fusion.2
  19.6 24.1 %collective-permute-done = bf16[70,3,3,896]{3,0,2,1:T(8,128)(2,1)S(1)} collective-permute-done((bf16[70,3,3,896]{3,0,2,1:T(8,128)(2,1)}, bf16[70,3,3,896]{3,0,2,1:T(8,128)(2,1)S(1)}, u32[]{:S(2)}, u32[]{:S(2)}) %collective-permute-start) | collective-permute-done | bytes 1128992 | tf_op jit(solution)/shard_map/ppermute | solution.py:20
  44.2 4.9 copy.47
  49.1 7.4 %gather_fusion = f32[86,3,3,896]{3,2,1,0:T(4,128)} fusion(f32[140,3,3,896]{3,2,1,0:T(4,128)} %copy.47, s32[1024]{0:T(1024)S(1)} %pad_clamp_fusion.1), kind=kCustom, calls=%fused_computation | custom fusion | bytes 5548376 | tf_op jit(solution)/shard_map/jit(_take)/gather | solution.py:64
  56.6 3.0 broadcast_select_fusion
  59.6 1.9 copy-done.1
  61.5 1.0 fusion.16
  65.5 8.8 %gather_fusion.1 = bf16[2752,256]{1,0:T(8,128)(2,1)} fusion(bf16[256,2048]{0,1:T(8,128)(2,1)S(1)} %copy.50, s32[3072]{0:T(1024)S(1)} %pad_clamp_fusion), kind=kCustom, calls=%fused_computation.1 | custom fusion | bytes 2829056 | tf_op jit(solution)/shard_map/jit(_take)/gather | solution.py:105
  74.3 8.5 %gather_fusion.2 = bf16[2752,256]{1,0:T(8,128)(2,1)S(1)} fusion(bf16[256,2048]{0,1:T(8,128)(2,1)S(1)} %copy.51, s32[3072]{0:T(1024)S(1)} %pad_clamp_fusion), kind=kCustom, calls=%fused_computation.2 | custom fusion | bytes 2829056 | tf_op jit(solution)/shard_map/jit(_take)/gather | solution.py:78
  82.9 134.0 %all-gather.2.cloned.1.call-done = bf16[2752,3,896]{2,1,0:T(4,128)(2,1)} async-done(((bf16[86,3,896]{2,1,0:T(4,128)(2,1)}), bf16[2752,3,896]{2,1,0:T(4,128)(2,1)}) %all-gather.2.cloned.1.call-update) | async-done | bytes 14794768 | tf_op jit(solution)/shard_map/all_gather | solution.py:73
  216.8 12.4 %copy_select_fusion = bf16[2752,3,896]{2,0,1:T(8,128)(2,1)S(1)} fusion(bf16[2752,3,896]{2,1,0:T(4,128)(2,1)} %all-gather.2.cloned.1.call-done, pred[2752]{0:T(1024)(128)(4,1)S(1)} %fusion.21), kind=kLoop, calls=%fused_computation.6 | loop fusion | flops 7397376 | bytes 29592256 | tf_op jit(solution)/shard_map/jit(_where)/select_n | solution.py:76
  229.2 1.7 fusion.10
  230.9 1.8 multiply_convert_fusion
  232.8 1.7 copy-done
  234.5 1.7 fusion.8
  236.2 1.8 multiply_bitcast_fusion.1
  238.0 1.8 multiply_bitcast_fusion.2
  239.8 1.6 multiply_bitcast_fusion
  241.4 7.7 %fusion = bf16[2752,3,896]{2,0,1:T(8,128)(2,1)} fusion(bf16[2752,1,896]{2,0,1:T(8,128)(2,1)S(1)} %multiply_bitcast_fusion, bf16[2752,1,896]{2,0,1:T(8,128)(2,1)S(1)} %multiply_bitcast_fusion.1, bf16[2752,1,896]{2,0,1:T(8,128)(2,1)S(1)} %multiply_bitcast_fusion.2, pred[2752]{0:T(1024)(128)(4,1)S(1)} %fusion.21), kind=kLoop, calls=%fused_computation.5 | loop fusion | flops 51781632 | bytes 29592256 | tf_op jit(solution)/shard_map/convert_element_type | solution.py:121
  249.2 18.7 %scatter_custom_fusion = bf16[2048,896]{1,0:T(8,128)(2,1)} fusion(s32[2752]{0:T(1024)S(1)} %get-tuple-element.16, bf16[2752,3,896]{2,0,1:T(8,128)(2,1)} %copy-done, bf16[]{:T(256)} %constant.32.clone.1), kind=kCustom, calls=%fused_computation.16 | custom fusion | bytes 8602112 | tf_op jit(solution)/shard_map/scatter | solution.py:83
  267.9 4.6 fusion.6
  273.8 269.6 %all-reduce.3.cloned.1.call-done = bf16[2752,3,896]{2,0,1:T(8,128)(2,1)} async-done(((bf16[2752,3,896]{2,0,1:T(8,128)(2,1)}), bf16[2752,3,896]{2,0,1:T(8,128)(2,1)}) %all-reduce.3.cloned.1.call-update) | async-done | bytes 14794768
  543.4 1.2 constant_dynamic-slice_fusion
  544.5 3.8 multiply_subtract_fusion
  548.3 1.0 copy.54
  549.3 1.0 copy.55
  550.3 1.0 copy.56
  551.3 28.9 %reduce-scatter.3.cloned.1.call-done = bf16[256,256]{1,0:T(8,128)(2,1)} async-done(((bf16[256,2048]{1,0:T(8,128)(2,1)}), bf16[256,256]{1,0:T(8,128)(2,1)}) %reduce-scatter.3.cloned.1.call-update) | async-done | bytes 131088 | tf_op jit(solution)/shard_map/reduce_scatter | solution.py:97
  (40 shorter events, 4.2 us)
Async XLA Ops:
  7.2 36.7 %copy-start.4 = (f32[70,3,896]{2,0,1:T(8,128)S(1)}, f32[70,3,896]{2,0,1:T(8,128)}, u32[]{:S(2)}) copy-start(f32[70,3,896]{2,0,1:T(8,128)} %param.9) | copy-start | bytes 2257924
  7.2 36.7 %copy-start.3 = (f32[70,3,896]{2,0,1:T(8,128)S(1)}, f32[70,3,896]{2,0,1:T(8,128)}, u32[]{:S(2)}) copy-start(f32[70,3,896]{2,0,1:T(8,128)} %param.10) | copy-start | bytes 2257924
  7.2 36.7 %copy-start.2 = (f32[70,3,896]{2,0,1:T(8,128)S(1)}, f32[70,3,896]{2,0,1:T(8,128)}, u32[]{:S(2)}) copy-start(f32[70,3,896]{2,0,1:T(8,128)} %param.11) | copy-start | bytes 2257924
  7.2 209.7 %all-gather.2.cloned.1.call-start = ((), (), s32[]{:S(2)}) async-start(), calls=%async_computation.1 | async-start | bytes 20342784 | tf_op jit(solution)/shard_map/all_gather | solution.py:73
  10.2 33.4 %collective-permute-start = (bf16[70,3,3,896]{3,0,2,1:T(8,128)(2,1)}, bf16[70,3,3,896]{3,0,2,1:T(8,128)(2,1)S(1)}, u32[]{:S(2)}, u32[]{:S(2)}) collective-permute-start(bf16[70,3,3,896]{3,0,2,1:T(8,128)(2,1)} %maximum_convert_fusion), channel_id=1, source_target_pairs={{0,8},{8,16},{16,24},{24,32},{32,40},{40,48},{48,56},{56,64},{64,7... | collective-permute-start | bytes 3386888 | tf_op jit(solution)/shard_map/ppermute | solution.py:20
  56.6 7.4 %copy-start.7 = (bf16[256,2048]{1,0:T(8,128)(2,1)S(1)}, bf16[256,2048]{1,0:T(8,128)(2,1)}, u32[]{:S(2)}) copy-start(bf16[256,2048]{1,0:T(8,128)(2,1)} %param.7) | copy-start | bytes 3145732
  59.6 1.9 copy-start.1
  61.5 3.0 copy-start.6
  62.5 2.6 copy-start.8
  62.6 480.8 %all-reduce.3.cloned.1.call-start = ((), (), s32[]{:S(2)}) async-start(), calls=%async_computation.3 | async-start | bytes 29589504
  82.9 146.3 %copy-start.5 = (bf16[2752,256]{1,0:T(8,128)(2,1)S(1)}, bf16[2752,256]{1,0:T(8,128)(2,1)}, u32[]{:S(2)}) copy-start(bf16[2752,256]{1,0:T(8,128)(2,1)} %gather_fusion.1) | copy-start | bytes 4227076
  229.2 5.3 copy-start
  249.2 331.1 %reduce-scatter.3.cloned.1.call-start = ((), (), s32[]{:S(2)}) async-start(), calls=%async_computation.2 | async-start | bytes 1179648 | tf_op jit(solution)/shard_map/reduce_scatter | solution.py:97
  267.9 4.6 copy-start.9
Sparse Core Ops, SparseCore 0:
  62.7 154.1 all-gather.1
  249.3 294.0 all-reduce.2
  546.5 33.7 reduce-scatter.2
where the time goes:
time: 587 us
  waiting for transfers between devices  457 us (78%)
  local copies, waits for them, and re-layouts  59.7 us (10%)
  other arithmetic  34.3 us (6%)
  between operations  17.3 us (3%)
  matrix products  15 us (3%)
    unnamed x4, waiting for transfers between devices  270 us
    all_gather x1, waiting for transfers between devices, train_pass(): shard_piece = lax.all_gather(weights, 'dp', axis=0, tiled=True)  134 us
    reduce_scatter x1, waiting for transfers between devices, train_pass(): lax.psum_scatter(partial_value.astype(jnp.bfloat16), 'mp', scatter_dimens...  28.9 us
    ppermute x1, waiting for transfers between devices, passed_along(): return lax.ppermute(value, axis, pairs)  24.1 us
    scatter x1, local copies, waits for them, and re-layouts, train_pass(): down_rows = down_rows.at[placed].set(shard_piece[:, 2], mode='drop')  18.7 us
    select_n x1, other arithmetic, train_pass(): jnp.where(in_range[:, None, None], shard_piece, jnp.zeros_like(shard_piece))  12.4 us
  transfers between devices with their start and end apart: 4, of which 4 were waited for; matrix products, arithmetic and copies ran while one was open for 9% of the time, Pallas kernels for 0%

commit v1 on v0

--- a/solution.py
+++ b/solution.py
@@ -70,7 +70,9 @@
     scale_in = FEATURE_WIDTH ** (-0.5)
     scale_hidden = FF ** (-0.5)
     contract_rows = (((0,), (0,)), ((), ()))
-    shard_piece = lax.all_gather(weights, "dp", axis=0, tiled=True)
+    shard_piece = jnp.concatenate(
+        lax.all_to_all(jnp.stack([weights] * lax.axis_size("dp")), "dp", 0, 0), axis=0
+    )
     down_rows = jnp.zeros((FEATURE_WIDTH, columns), jnp.bfloat16)
     target, in_range = row_layout(shard_piece.shape[0], capacity, layout)
     shard_piece = jnp.where(in_range[:, None, None], shard_piece, jnp.zeros_like(shard_piece))

time: 587 us -> 812 us (1.38)
  waiting for transfers between devices: 457 us -> 634 us
  local copies, waits for them, and re-layouts: 59.7 us -> 98.5 us
  starting transfers between devices: 3.93 us -> 13.2 us
    all_to_all x0 -> x1, waiting for transfers between devices: none -> 324 us  [train_pass(): lax.all_to_all(jnp.stack([weights] * lax.axis_size('dp')), 'dp', 0, 0)]
    all_gather x1 -> x0, waiting for transfers between devices: 134 us -> none  [train_pass(): shard_piece = lax.all_gather(weights, 'dp', axis=0, tiled=True)]
    reduce_scatter x1, waiting for transfers between devices: 28.9 us -> 0.01 us  [train_pass(): lax.psum_scatter(partial_value.astype(jnp.bfloat16), 'mp', scatter_dimens...]
    reshape x0 -> x1, local copies, waits for them, and re-layouts: none -> 19.6 us  [train_pass(): jnp.concatenate(lax.all_to_all(jnp.stack([weights] * lax.axis_size('dp'))...]
    unnamed x4 -> x3, waiting for transfers between devices: 270 us -> 287 us
    all_to_all x0 -> x1, local copies, waits for them, and re-layouts: none -> 13.6 us  [train_pass(): lax.all_to_all(jnp.stack([weights] * lax.axis_size('dp')), 'dp', 0, 0)]
    all_to_all x0 -> x1, starting transfers between devices: none -> 9.09 us  [train_pass(): lax.all_to_all(jnp.stack([weights] * lax.axis_size('dp')), 'dp', 0, 0)]
  transfers between devices with their start and end apart: 4 -> 4, of which waited for: 4 -> 3; matrix products, arithmetic and copies ran while one was open for 9% -> 7% of each run, Pallas kernels for 0% -> 0%
where the time goes in v1:
time: 812 us; the launch traced here: 810 us
  waiting for transfers between devices  634 us (78%)
  local copies, waits for them, and re-layouts  98.5 us (12%)
  other arithmetic  30.1 us (4%)
  between operations  19.1 us (2%)
  matrix products  14.9 us (2%)
  starting transfers between devices  13.2 us (2%)
    all_to_all x1, waiting for transfers between devices, train_pass(): lax.all_to_all(jnp.stack([weights] * lax.axis_size('dp')), 'dp', 0, 0)  324 us
    unnamed x3, waiting for transfers between devices  287 us
    ppermute x1, waiting for transfers between devices, passed_along(): return lax.ppermute(value, axis, pairs)  24.1 us
    reshape x1, local copies, waits for them, and re-layouts, train_pass(): jnp.concatenate(lax.all_to_all(jnp.stack([weights] * lax.axis_size('dp'))...  19.6 us
    scatter x1, local copies, waits for them, and re-layouts, train_pass(): down_rows = down_rows.at[placed].set(shard_piece[:, 2], mode='drop')  18.7 us
  transfers between devices with their start and end apart: 4, of which 3 were waited for; matrix products, arithmetic and copies ran while one was open for 7% of the time, Pallas kernels for 0%

profile of v1, /device:TPU:8, one launch (start us, length us, event | category | flops | bytes accessed | tf_op | source)
XLA Modules:
  0.0 810.2 jit_solution(15133640959747882339)
XLA Ops:
  8.0 3.0 maximum_convert_fusion
  11.0 3.8 collective-permute-start
  15.6 1.3 fusion.27
  20.4 24.1 %collective-permute-done = bf16[70,3,3,896]{3,0,2,1:T(8,128)(2,1)S(1)} collective-permute-done((bf16[70,3,3,896]{3,0,2,1:T(8,128)(2,1)}, bf16[70,3,3,896]{3,0,2,1:T(8,128)(2,1)S(1)}, u32[]{:S(2)}, u32[]{:S(2)}) %collective-permute-start) | collective-permute-done | bytes 1128992 | tf_op jit(solution)/shard_map/ppermute | solution.py:20
  45.0 4.9 copy.49
  49.9 7.4 gather_fusion
  57.4 2.9 broadcast_select_fusion.1
  60.3 1.9 copy-done.1
  62.5 6.5 stack.22
  68.9 9.1 %all-to-all-start = ((bf16[32,86,3,896]{3,1,2,0:T(8,128)(2,1)}), bf16[32,86,3,896]{3,1,2,0:T(8,128)(2,1)}, u32[]{:S(2)}, u32[]{:S(2)}) async-start(bf16[32,86,3,896]{3,1,2,0:T(8,128)(2,1)} %stack.22), calls=%async_computation | async-start | bytes 30277632 | tf_op jit(solution)/shard_map/all_to_all | solution.py:74
  81.1 8.9 %gather_fusion.1 = bf16[2752,256]{1,0:T(8,128)(2,1)} fusion(bf16[256,2048]{0,1:T(8,128)(2,1)S(1)} %copy.52, s32[3072]{0:T(1024)S(1)} %pad_clamp_fusion), kind=kCustom, calls=%fused_computation.1 | custom fusion | bytes 2829056 | tf_op jit(solution)/shard_map/jit(_take)/gather | solution.py:107
  90.0 8.5 %gather_fusion.2 = bf16[2752,256]{1,0:T(8,128)(2,1)S(1)} fusion(bf16[256,2048]{0,1:T(8,128)(2,1)S(1)} %copy.53, s32[3072]{0:T(1024)S(1)} %pad_clamp_fusion), kind=kCustom, calls=%fused_computation.2 | custom fusion | bytes 2829056 | tf_op jit(solution)/shard_map/jit(_take)/gather | solution.py:80
  98.5 323.9 %all-to-all-done = bf16[32,86,3,896]{3,1,2,0:T(8,128)(2,1)} async-done(((bf16[32,86,3,896]{3,1,2,0:T(8,128)(2,1)}), bf16[32,86,3,896]{3,1,2,0:T(8,128)(2,1)}, u32[]{:S(2)}, u32[]{:S(2)}) %all-to-all-start) | async-done | bytes 14794784 | tf_op jit(solution)/shard_map/all_to_all | solution.py:74
  422.4 13.6 %copy.55 = bf16[32,86,3,896]{3,1,0,2:T(8,128)(2,1)} copy(bf16[32,86,3,896]{3,1,2,0:T(8,128)(2,1)} %all-to-all-done) | data formatting | bytes 29589504 | tf_op jit(solution)/shard_map/all_to_all | solution.py:74
  436.0 19.6 %reshape.174 = bf16[2752,3,896]{2,0,1:T(8,128)(2,1)} reshape(bf16[32,86,3,896]{3,1,0,2:T(8,128)(2,1)} %copy.55) | data formatting | bytes 29589504 | tf_op jit(solution)/shard_map/reshape | solution.py:73
  455.6 8.3 %broadcast_select_fusion = bf16[2752,3,896]{2,0,1:T(8,128)(2,1)S(1)} fusion(bf16[2752,3,896]{2,0,1:T(8,128)(2,1)} %reshape.174, pred[2752]{0:T(1024)(128)(4,1)S(1)} %fusion.21), kind=kLoop, calls=%fused_computation.6 | loop fusion | flops 7397376 | bytes 29592256 | tf_op jit(solution)/shard_map/jit(_where)/select_n | solution.py:78
  463.9 1.7 fusion.10
  465.6 1.8 multiply_convert_fusion
  467.5 1.7 copy-done
  469.2 1.7 fusion.8
  470.9 1.8 multiply_bitcast_fusion.1
  472.6 1.8 multiply_bitcast_fusion.2
  474.5 1.6 multiply_bitcast_fusion
  476.1 7.7 fusion
  483.9 18.7 %scatter_custom_fusion = bf16[2048,896]{1,0:T(8,128)(2,1)} fusion(s32[2752]{0:T(1024)S(1)} %get-tuple-element.16, bf16[2752,3,896]{2,0,1:T(8,128)(2,1)} %copy-done, bf16[]{:T(256)} %constant.32.clone.1), kind=kCustom, calls=%fused_computation.16 | custom fusion | bytes 8602112 | tf_op jit(solution)/shard_map/scatter | solution.py:85
  502.6 4.5 fusion.6
  508.3 286.5 %all-reduce.3.cloned.1.call-done = bf16[2752,3,896]{2,0,1:T(8,128)(2,1)} async-done(((bf16[2752,3,896]{2,0,1:T(8,128)(2,1)}), bf16[2752,3,896]{2,0,1:T(8,128)(2,1)}) %all-reduce.3.cloned.1.call-update) | async-done | bytes 14794768
  794.8 1.2 constant_dynamic-slice_fusion
  796.0 3.8 multiply_subtract_fusion
  799.8 1.0 copy.57
  800.8 1.0 copy.58
  801.8 1.0 copy.59
  (43 shorter events, 6.1 us)
Async XLA Ops:
  8.0 36.6 %copy-start.4 = (f32[70,3,896]{2,0,1:T(8,128)S(1)}, f32[70,3,896]{2,0,1:T(8,128)}, u32[]{:S(2)}) copy-start(f32[70,3,896]{2,0,1:T(8,128)} %param.9) | copy-start | bytes 2257924
  8.0 36.6 %copy-start.3 = (f32[70,3,896]{2,0,1:T(8,128)S(1)}, f32[70,3,896]{2,0,1:T(8,128)}, u32[]{:S(2)}) copy-start(f32[70,3,896]{2,0,1:T(8,128)} %param.10) | copy-start | bytes 2257924
  8.0 36.6 %copy-start.2 = (f32[70,3,896]{2,0,1:T(8,128)S(1)}, f32[70,3,896]{2,0,1:T(8,128)}, u32[]{:S(2)}) copy-start(f32[70,3,896]{2,0,1:T(8,128)} %param.11) | copy-start | bytes 2257924
  11.0 33.4 %collective-permute-start = (bf16[70,3,3,896]{3,0,2,1:T(8,128)(2,1)}, bf16[70,3,3,896]{3,0,2,1:T(8,128)(2,1)S(1)}, u32[]{:S(2)}, u32[]{:S(2)}) collective-permute-start(bf16[70,3,3,896]{3,0,2,1:T(8,128)(2,1)} %maximum_convert_fusion), channel_id=1, source_target_pairs={{0,8},{8,16},{16,24},{24,32},{32,40},{40,48},{48,56},{56,64},{64,7... | collective-permute-start | bytes 3386888 | tf_op jit(solution)/shard_map/ppermute | solution.py:20
  60.3 1.9 copy-start.1
  68.9 10.6 %copy-start.7 = (bf16[256,2048]{1,0:T(8,128)(2,1)S(1)}, bf16[256,2048]{1,0:T(8,128)(2,1)}, u32[]{:S(2)}) copy-start(bf16[256,2048]{1,0:T(8,128)(2,1)} %param.7) | copy-start | bytes 3145732
  68.9 11.2 %copy-start.6 = (bf16[256,2048]{1,0:T(8,128)(2,1)S(1)}, bf16[256,2048]{1,0:T(8,128)(2,1)}, u32[]{:S(2)}) copy-start(bf16[256,2048]{1,0:T(8,128)(2,1)} %param.8) | copy-start | bytes 3145732
  68.9 353.5 %all-to-all-start = ((bf16[32,86,3,896]{3,1,2,0:T(8,128)(2,1)}), bf16[32,86,3,896]{3,1,2,0:T(8,128)(2,1)}, u32[]{:S(2)}, u32[]{:S(2)}) async-start(bf16[32,86,3,896]{3,1,2,0:T(8,128)(2,1)} %stack.22), calls=%async_computation | async-start | bytes 30277632 | tf_op jit(solution)/shard_map/all_to_all | solution.py:74
  78.0 2.7 copy-start.8
  78.0 716.8 %all-reduce.3.cloned.1.call-start = ((), (), s32[]{:S(2)}) async-start(), calls=%async_computation.3 | async-start | bytes 29589504
  455.6 8.3 %copy-start.5 = (bf16[2752,256]{1,0:T(8,128)(2,1)S(1)}, bf16[2752,256]{1,0:T(8,128)(2,1)}, u32[]{:S(2)}) copy-start(bf16[2752,256]{1,0:T(8,128)(2,1)} %gather_fusion.1) | copy-start | bytes 4227076
  463.9 5.3 copy-start
  483.8 318.9 %reduce-scatter.3.cloned.1.call-start = ((), (), s32[]{:S(2)}) async-start(), calls=%async_computation.2 | async-start | bytes 1179648 | tf_op jit(solution)/shard_map/reduce_scatter | solution.py:99
  502.6 4.5 copy-start.9
Sparse Core Ops, SparseCore 0:
  484.0 310.8 all-reduce.2
Sparse Core Ops, SparseCore 1:
  507.2 50.4 reduce-scatter.2
